TPU v7x, 32 devices: a whole 2x2x4 slice. The times are simulated.
32 devices in a mesh: node: 8 (over z, core), local: 4 (over y, x).
Axes of the slice: x: 2, y: 2, z: 4, core: 2. Of those that a mesh axis runs over, the one named last changes fastest.
Arguments:
- grad_out: bfloat16 [512, 4096], P(('node', 'local')), may hold values from -6 to 6
- gate_pre: bfloat16 [512, 14592], P('node', 'local'), may hold values from -6 to 6
- up_pre: bfloat16 [512, 14592], P('node', 'local'), may hold values from -6 to 6
- w_down: bfloat16 [14592, 4096], P('local'), may hold values from -0.046875 to 0.046875
Outputs:
- grad_gate: bfloat16 [512, 14592], P('node', 'local')
- grad_up: bfloat16 [512, 14592], P('node', 'local')
- grad_weight: float32 [14592, 4096], P(('local', 'node'))
All inputs are finite; a program needn't handle non-finite values.
Results may differ from a plain program's by a relative error of at most 0.0029.
Values may be sent and summed in bfloat16 or wider, within the bound.
A program may use at most 192 MiB of HBM per device.

v0:
```python
import jax
import jax.numpy as jnp
from jax import lax
from jax.sharding import PartitionSpec as P


def on_device(grad_out, gate_pre, up_pre, w_down):
    gate = gate_pre.astype(jnp.float32)
    up = up_pre.astype(jnp.float32)
    sig = jax.nn.sigmoid(gate)
    act = gate * sig
    hidden = (act * up).astype(jnp.bfloat16)
    node_grad = lax.all_gather(grad_out, "local", axis=0, tiled=True)
    grad_hidden = jnp.einsum("td,fd->tf", node_grad, w_down, preferred_element_type=jnp.float32)
    grad_up = (grad_hidden * act).astype(jnp.bfloat16)
    grad_gate = (grad_hidden * up * sig * (1.0 + gate * (1.0 - sig))).astype(jnp.bfloat16)
    partial_value = jnp.einsum("tf,td->fd", hidden, node_grad, preferred_element_type=jnp.float32)
    grad_weight = lax.psum_scatter(partial_value, "node", scatter_dimension=0, tiled=True)
    return (grad_gate, grad_up, grad_weight)


def solution(mesh):
    return jax.shard_map(
        on_device,
        mesh=mesh,
        in_specs=(
            P(("node", "local"), None),
            P("node", "local"),
            P("node", "local"),
            P("local", None),
        ),
        out_specs=(P("node", "local"), P("node", "local"), P(("local", "node"), None)),
        check_vma=False,
    )
```

profile of v0, /device:TPU:0, one launch (start us, length us, event | category | flops | bytes accessed | tf_op | source)
XLA Modules:
  0.0 622.2 jit_solution(14798417014237629114)
XLA Ops:
  7.2 0.0 reduce-scatter.4.cloned.1.call-start
  7.2 11.8 %all_gather.3 = bf16[64,4096]{1,0:T(8,128)(2,1)S(1)} all-gather(bf16[16,4096]{1,0:T(8,128)(2,1)} %param.4), channel_id=1, replica_groups=mesh['node'=8,'local'=4] {'local'}, dimensions={0}, use_global_device_ids=true | all-gather | bytes 655360 | tf_op jit(solution)/shard_map/all_gather | solution.py:13
  19.1 24.1 %fusion.8 = f32[3648,4096]{1,0:T(8,128)} fusion(bf16[64,4096]{1,0:T(8,128)(2,1)S(1)} %all_gather.3, bf16[64,3648]{1,0:T(8,128)(2,1)} %param.6, bf16[64,3648]{1,0:T(8,128)(2,1)} %param.5), kind=kOutput, calls=%fused_computation.14 | convolution fusion | flops 1914470400 | bytes 61227008 | tf_op jit(solution)/shard_map/tf,td->fd/dot_general | solution.py:17
  43.2 0.0 copy-start
  43.2 0.0 copy-start.1
  43.2 0.0 reduce-scatter.4.cloned.1.call-update
  43.2 1.0 copy-done
  44.2 0.1 copy-done.1
  44.3 15.9 %multiply_convert_fusion = (bf16[64,3648]{1,0:T(8,128)(2,1)}, bf16[64,3648]{1,0:T(8,128)(2,1)}) fusion(bf16[64,3648]{1,0:T(8,128)(2,1)S(1)} %copy-done, bf16[64,3648]{1,0:T(8,128)(2,1)S(1)} %copy-done.1, bf16[64,4096]{1,0:T(8,128)(2,1)S(1)} %all_gather.3, bf16[3648,4096]{1,0:T(8,128)(2,1)} %param.7), kind=kOutput, calls=%fused_computation.13 | convolution fusion | flops 1916104704 | bytes 32276480 | tf_op jit(solution)/shard_map/td,fd->tf/dot_general | solution.py:14
  60.3 555.1 %reduce-scatter.4.cloned.1.call-done = f32[456,4096]{1,0:T(8,128)} async-done(((f32[3648,4096]{1,0:T(8,128)}), f32[456,4096]{1,0:T(8,128)}) %reduce-scatter.4.cloned.1.call-update) | async-done | bytes 7471120
Async XLA Ops:
  7.2 608.2 %reduce-scatter.4.cloned.1.call-start = ((), (), s32[]{:S(2)}) async-start(), calls=%async_computation.1 | async-start | bytes 67239936
  43.2 1.0 copy-start
  43.2 1.2 copy-start.1
Sparse Core Ops, SparseCore 0:
  43.3 572.0 reduce-scatter.3
where the time goes:
time: 622 us
  waiting for transfers between devices  555 us (89%)
  matrix products  40.1 us (6%)
  between operations  14 us (2%)
  blocking collectives  11.8 us (2%)
    unnamed x2, waiting for transfers between devices  555 us
    dot_general x1, matrix products, on_device(): jnp.einsum('tf,td->fd', hidden, node_grad, preferred_element_type=jnp.flo...  24.1 us
    dot_general x1, matrix products, on_device(): jnp.einsum('td,fd->tf', node_grad, w_down, preferred_element_type=jnp.flo...  15.9 us
  transfers between devices with their start and end apart: 1, of which 1 were waited for; matrix products, arithmetic and copies ran while one was open for 3% of the time, Pallas kernels for 0%

commit v1 on v0

--- a/solution.py
+++ b/solution.py
@@ -4,11 +4,15 @@
 from jax.sharding import PartitionSpec as P
 
 
-def on_device(grad_out, gate_pre, up_pre, w_down):
+def factors(gate_pre, up_pre):
     gate = gate_pre.astype(jnp.float32)
     up = up_pre.astype(jnp.float32)
     sig = jax.nn.sigmoid(gate)
-    act = gate * sig
+    return gate, up, sig, gate * sig
+
+
+def summed(grad_out, gate_pre, up_pre, w_down):
+    gate, up, sig, act = factors(gate_pre, up_pre)
     hidden = (act * up).astype(jnp.bfloat16)
     node_grad = lax.all_gather(grad_out, "local", axis=0, tiled=True)
     grad_hidden = jnp.einsum("td,fd->tf", node_grad, w_down, preferred_element_type=jnp.float32)
@@ -19,7 +23,29 @@
     return (grad_gate, grad_up, grad_weight)
 
 
+def gathered(grad_out, gate_pre, up_pre, w_down):
+    gate, up, sig, act = factors(gate_pre, up_pre)
+    hidden = (act * up).astype(jnp.bfloat16)
+    mine = lax.all_to_all(hidden, "node", split_axis=1, concat_axis=0, tiled=True)
+    all_grad = lax.all_gather(grad_out, ("node", "local"), axis=0, tiled=True)
+    tokens = gate_pre.shape[0]
+    node_grad = lax.dynamic_slice_in_dim(all_grad, lax.axis_index("node") * tokens, tokens, 0)
+    grad_hidden = jnp.einsum("td,fd->tf", node_grad, w_down, preferred_element_type=jnp.float32)
+    grad_up = (grad_hidden * act).astype(jnp.bfloat16)
+    grad_gate = (grad_hidden * up * sig * (1.0 + gate * (1.0 - sig))).astype(jnp.bfloat16)
+    grad_weight = jnp.einsum("tf,td->fd", mine, all_grad, preferred_element_type=jnp.float32)
+    return (grad_gate, grad_up, grad_weight)
+
+
 def solution(mesh):
+    devices = mesh.shape["node"] * mesh.shape["local"]
+
+    def on_device(grad_out, gate_pre, up_pre, w_down):
+        gather_bytes = devices * grad_out.size * 2
+        sum_bytes = w_down.size * 4
+        plan = gathered if gather_bytes < sum_bytes else summed
+        return plan(grad_out, gate_pre, up_pre, w_down)
+
     return jax.shard_map(
         on_device,
         mesh=mesh,

time: 622 us -> 125 us (0.20)
  waiting for transfers between devices: 555 us -> 68.4 us
  matrix products: 40.1 us -> 22.6 us
  blocking collectives: 11.8 us -> 18.3 us
    unnamed x2 -> x1, waiting for transfers between devices: 555 us -> 0.68 us
    all_gather x0 -> x1, waiting for transfers between devices: none -> 67.7 us  [gathered(): all_grad = lax.all_gather(grad_out, ('node', 'local'), axis=0, tiled=True)]
    all_to_all x0 -> x1, blocking collectives: none -> 18.3 us  [gathered(): lax.all_to_all(hidden, 'node', split_axis=1, concat_axis=0, tiled=True)]
    dot_general x2, matrix products: 40.1 us -> 22.6 us  [the longest x1 15.2 us: gathered(): jnp.einsum('td,fd->tf', node_grad, w_down, preferred_element_type=jnp.flo...]
    all_gather x1 -> x0, blocking collectives: 11.8 us -> none  [on_device(): node_grad = lax.all_gather(grad_out, 'local', axis=0, tiled=True)]
  transfers between devices with their start and end apart: 1 -> 1, of which waited for: 1 -> 1; matrix products, arithmetic and copies ran while one was open for 3% -> 0% of each run, Pallas kernels for 0% -> 0%
where the time goes in v1:
time: 125 us
  waiting for transfers between devices  68.4 us (55%)
  matrix products  22.6 us (18%)
  blocking collectives  18.3 us (15%)
  between operations  14 us (11%)
  local copies, waits for them, and re-layouts  1.35 us (1%)
    all_gather x1, waiting for transfers between devices, gathered(): all_grad = lax.all_gather(grad_out, ('node', 'local'), axis=0, tiled=True)  67.7 us
    all_to_all x1, blocking collectives, gathered(): lax.all_to_all(hidden, 'node', split_axis=1, concat_axis=0, tiled=True)  18.3 us
    dot_general x1, matrix products, gathered(): jnp.einsum('td,fd->tf', node_grad, w_down, preferred_element_type=jnp.flo...  15.2 us
    dot_general x1, matrix products, gathered(): jnp.einsum('tf,td->fd', mine, all_grad, preferred_element_type=jnp.float32)  7.45 us
  transfers between devices with their start and end apart: 1, of which 1 were waited for; matrix products, arithmetic and copies ran while one was open for 0% of the time, Pallas kernels for 0%

profile of v1, /device:TPU:0, one launch (start us, length us, event | category | flops | bytes accessed | tf_op | source)
XLA Modules:
  0.0 124.8 jit_solution(3103934168967584631)
XLA Ops:
  7.2 0.0 all-gather.2.cloned.1.call-start
  7.2 0.7 all-gather.2.cloned.1.call-update
  7.9 67.7 %all-gather.2.cloned.1.call-done = bf16[512,4096]{1,0:T(8,128)(2,1)} async-done(((bf16[16,4096]{1,0:T(8,128)(2,1)}), bf16[512,4096]{1,0:T(8,128)(2,1)}) %all-gather.2.cloned.1.call-update) | async-done | bytes 4194320 | tf_op jit(solution)/shard_map/all_gather | solution.py:30
  75.6 15.2 %multiply_convert_fusion = (bf16[64,3648]{1,0:T(8,128)(2,1)}, bf16[64,3648]{1,0:T(8,128)(2,1)}, bf16[64,3648]{1,0:T(8,128)(2,1)S(1)}) fusion(bf16[64,3648]{1,0:T(8,128)(2,1)} %param.5, bf16[64,3648]{1,0:T(8,128)(2,1)} %param.6, bf16[3648,4096]{1,0:T(8,128)(2,1)} %param.7, bf16[512,4096]{1,0:T(8,128)(2,1)} %all-gather.2.cloned.1.call-done, s32[]{:T(128)S(6)} %select_n.3), kind=kOutput, calls=%fused_computation.13 | convolution fusion | flops 1916571648 | bytes 32759812 | tf_op jit(solution)/shard_map/td,fd->tf/dot_general | solution.py:33
  90.8 1.2 all_to_all.14
  92.0 0.2 copy.7
  92.2 18.3 %all_to_all.19 = bf16[64,8,456]{2,0,1:T(8,128)(2,1)S(1)} all-to-all(bf16[64,8,456]{2,0,1:T(8,128)(2,1)S(1)} %copy.7), channel_id=1, replica_groups=mesh['node'=8,'local'=4] {'node'}, dimensions={1} | all-to-all | bytes 933888 | tf_op jit(solution)/shard_map/all_to_all | solution.py:29
  110.5 7.5 %fusion.11 = f32[456,4096]{1,0:T(8,128)} fusion(bf16[512,456]{1,0:T(8,128)(2,1)S(1)} %bitcast.6, bf16[512,4096]{1,0:T(8,128)(2,1)} %all-gather.2.cloned.1.call-done), kind=kOutput, calls=%fused_computation.17 | convolution fusion | flops 1912602624 | bytes 12132352 | tf_op jit(solution)/shard_map/tf,td->fd/dot_general | solution.py:36
Async XLA Ops:
  7.2 68.5 %all-gather.2.cloned.1.call-start = ((), (), s32[]{:S(2)}) async-start(), calls=%async_computation.1 | async-start | bytes 4325376 | tf_op jit(solution)/shard_map/all_gather | solution.py:30
Sparse Core Ops, SparseCore 0:
  10.9 64.7 all-gather.1

commit v2 on v0

--- a/solution.py
+++ b/solution.py
@@ -1,14 +1,26 @@
+import functools
+
 import jax
 import jax.numpy as jnp
 from jax import lax
+from jax.experimental import pallas as pl
+from jax.experimental.pallas import tpu as pltpu
 from jax.sharding import PartitionSpec as P
 
-
-def on_device(grad_out, gate_pre, up_pre, w_down):
+MESH = pl.DeviceIdType.MESH
+LANES = 128
+STEP = 384
+
+
+def factors(gate_pre, up_pre):
     gate = gate_pre.astype(jnp.float32)
     up = up_pre.astype(jnp.float32)
     sig = jax.nn.sigmoid(gate)
-    act = gate * sig
+    return gate, up, sig, gate * sig
+
+
+def summed(grad_out, gate_pre, up_pre, w_down):
+    gate, up, sig, act = factors(gate_pre, up_pre)
     hidden = (act * up).astype(jnp.bfloat16)
     node_grad = lax.all_gather(grad_out, "local", axis=0, tiled=True)
     grad_hidden = jnp.einsum("td,fd->tf", node_grad, w_down, preferred_element_type=jnp.float32)
@@ -19,7 +31,306 @@
     return (grad_gate, grad_up, grad_weight)
 
 
+def exchange(nodes, go, gate, up, w, all_grad, all_hidden, gg, gu,
+             wv, ng, hf, hs, xs, xr, ys, yr, xhs, xhr, yhs, yhr, zs, zr, ss, sr, hss, hsr, ws, ls):
+    n, l = lax.axis_index("node"), lax.axis_index("local")
+    levels = nodes // 2
+    z, c = lax.div(n, 2), lax.rem(n, 2)
+    y, x = lax.div(l, 2), lax.rem(l, 2)
+    lx, ly, ld = y * 2 + 1 - x, (1 - y) * 2 + x, (1 - y) * 2 + 1 - x
+    xn, yn, sib = (n, lx), (n, ly), (z * 2 + 1 - c, l)
+    rows, width = go.shape
+    half = width // 2
+    tokens, hidden_units = gate.shape
+    block = hidden_units // nodes
+    padded = hs.shape[2]
+
+    starts = list(range(0, hidden_units, STEP))
+    full = hidden_units // STEP
+
+    def w_copy(i, size=STEP):
+        at = pl.ds(i * STEP if isinstance(i, int) else pl.multiple_of(i * STEP, STEP), size)
+        return pltpu.make_async_copy(w.at[at, :], wv.at[at, :], ws.at[i])
+
+    for i, start in enumerate(starts):
+        w_copy(i, min(STEP, hidden_units - start)).start()
+
+    barrier = pltpu.get_barrier_semaphore()
+    for peer in [xn, yn] + [(lax.rem(n + k, nodes), l) for k in range(1, nodes)]:
+        pl.semaphore_signal(barrier, inc=1, device_id=peer, device_id_type=MESH)
+    pl.semaphore_wait(barrier, nodes + 1)
+
+    def slot(level, core, local, part=None):
+        at = pl.ds(pl.multiple_of(((level * 2 + core) * 4 + local) * rows, rows), rows)
+        if part is None:
+            return all_grad.at[at, :]
+        return all_grad.at[at, pl.ds(part * half, half)]
+
+    def remote(source, target, sent, received, device):
+        return pltpu.make_async_remote_copy(
+            src_ref=source, dst_ref=target, send_sem=sent, recv_sem=received,
+            device_id=device, device_id_type=MESH)
+
+    def arrived(target, received):
+        remote(target, target, hss.at[0], received, xn).wait_recv()
+
+    start, sent = (lambda copy: copy.start()), (lambda copy: copy.wait_send())
+
+    def along(level, source, side, act):
+        can = z > 0 if side < 0 else z < levels - 1
+        to = (n + 2 * side, l)
+
+        @pl.when(can)
+        def _():
+            act(remote(source, slot(level, c, l), zs.at[(side + 1) // 2, level], zr.at[level], to))
+
+    def across(level, source, act):
+        target = slot(level, c, l)
+        act(remote(source, target, xs.at[level], xr.at[level], xn))
+        act(remote(source, target, ys.at[level], yr.at[level], yn))
+        act(remote(source, target, ss.at[level, l], sr.at[level, l], sib))
+
+    def from_x(level, act):
+        part, whole = slot(level, c, lx, 0), slot(level, c, lx)
+        act(remote(part, part, yhs.at[level], yhr.at[level], yn))
+        act(remote(whole, whole, ss.at[level, lx], sr.at[level, lx], sib))
+
+    def from_y(level, act):
+        part, whole = slot(level, c, ly, 1), slot(level, c, ly)
+        act(remote(part, part, xhs.at[level], xhr.at[level], xn))
+        act(remote(whole, whole, ss.at[level, ly], sr.at[level, ly], sib))
+
+    def from_d(level, act):
+        whole = slot(level, c, ld)
+        act(remote(whole, whole, ss.at[level, ld], sr.at[level, ld], sib))
+
+    def each(distance, run):
+        for side in (-1, 1):
+            level = z + side * distance
+
+            @pl.when((level >= 0) & (level < levels))
+            def _():
+                run(level, side)
+
+    def z_event(level, side):
+        arrived(slot(level, c, l), zr.at[level])
+        source = slot(level, c, l)
+        along(level, source, -side, start)
+        across(level, source, start)
+
+    def xy_event(level, side=0):
+        arrived(slot(level, c, lx), xr.at[level])
+        from_x(level, start)
+        arrived(slot(level, c, ly), yr.at[level])
+        from_y(level, start)
+
+    def d_event(level, side=0):
+        arrived(slot(level, c, ld, 0), yhr.at[level])
+        arrived(slot(level, c, ld, 1), xhr.at[level])
+        from_d(level, start)
+
+    for side in (-1, 1):
+        along(z, go, side, start)
+    across(z, go, start)
+    own = pltpu.make_async_copy(go, slot(z, c, l), ls.at[0])
+    own.start()
+
+    spread = hf.shape[1]
+    last = hidden_units // LANES * LANES
+    if spread > last:
+        hf[:, last:] = jnp.zeros((tokens, spread - last), jnp.float32)
+
+    @pl.loop(0, tokens // 16)
+    def _(i):
+        at = pl.ds(pl.multiple_of(i * 16, 16), 16)
+        for first in range(0, hidden_units, 512):
+            columns = slice(first, min(first + 512, hidden_units))
+            g = gate[at, columns].astype(jnp.float32)
+            hf[at, columns] = g * jax.nn.sigmoid(g) * up[at, columns].astype(jnp.float32)
+
+    @pl.loop(0, tokens // 16)
+    def _(i):
+        at = pl.ds(pl.multiple_of(i * 16, 16), 16)
+        for k in range(nodes):
+            base = k * block // LANES * LANES
+            shift = k * block - base
+            window = padded + (LANES if shift else 0)
+            values = hf[at, base:base + window]
+            if shift:
+                values = pltpu.roll(values, window - shift, 1)[:, :padded]
+            hs[k, at, :] = values.astype(jnp.bfloat16)
+
+    def hidden_copy(k):
+        to = lax.rem(n + k, nodes)
+        return remote(hs.at[to], all_hidden.at[n], hss.at[k], hsr.at[n], (to, l))
+
+    for k in range(1, nodes):
+        hidden_copy(k).start()
+    own_hidden = pltpu.make_async_copy(hs.at[n], all_hidden.at[n], ls.at[1])
+    own_hidden.start()
+
+    def multiply(i, size=STEP):
+        w_copy(i, size).wait()
+        at = pl.ds(i * STEP if isinstance(i, int) else pl.multiple_of(i * STEP, STEP), size)
+        grad = lax.dot_general(ng[...], wv[at, :], (((1,), (1,)), ((), ())),
+                               preferred_element_type=jnp.float32)
+        g, u = gate[:, at].astype(jnp.float32), up[:, at].astype(jnp.float32)
+        sig = jax.nn.sigmoid(g)
+        gu[:, at] = (grad * (g * sig)).astype(jnp.bfloat16)
+        gg[:, at] = (grad * u * sig * (1.0 + g * (1.0 - sig))).astype(jnp.bfloat16)
+
+    def multiply_some(part, parts):
+        first, stop = full * part // parts, full * (part + 1) // parts
+
+        @pl.loop(first, stop)
+        def _(i):
+            multiply(i)
+
+    xy_event(z)
+    if levels > 1:
+        each(1, z_event)
+    d_event(z)
+    own.wait()
+    node_rows = pl.ds(pl.multiple_of(n * tokens, tokens), tokens)
+    load = pltpu.make_async_copy(all_grad.at[node_rows, :], ng, ls.at[2])
+    load.start()
+    load.wait()
+    parts = 2 * levels - 1
+    for distance in range(1, levels):
+        multiply_some(2 * distance - 2, parts)
+        if distance + 1 < levels:
+            each(distance + 1, z_event)
+        each(distance, xy_event)
+        multiply_some(2 * distance - 1, parts)
+        each(distance, d_event)
+    multiply_some(parts - 1, parts)
+    if hidden_units % STEP:
+        multiply(full, hidden_units % STEP)
+
+    @pl.loop(0, levels)
+    def _(level):
+        for local in range(4):
+            arrived(slot(level, 1 - c, local), sr.at[level, local])
+
+    for k in range(1, nodes):
+        other = lax.rem(n + k, nodes)
+        arrived(all_hidden.at[other], hsr.at[other])
+        hidden_copy(k).wait_send()
+    own_hidden.wait()
+
+    def z_sent(level, side):
+        along(level, slot(level, c, l), -side, sent)
+
+    for side in (-1, 1):
+        along(z, go, side, sent)
+    for distance in range(1, levels):
+        each(distance, z_sent)
+
+    @pl.loop(0, levels)
+    def _(level):
+        across(level, slot(level, c, l), sent)
+        from_x(level, sent)
+        from_y(level, sent)
+        from_d(level, sent)
+
+
+def weight(hidden, grads, gg, gu, out, gg_out, gu_out, turned, sems):
+    copies = [pltpu.make_async_copy(gg, gg_out, sems.at[0]), pltpu.make_async_copy(gu, gu_out, sems.at[1])]
+    i = pl.program_id(0)
+
+    @pl.when(i == 0)
+    def _():
+        for copy in copies:
+            copy.start()
+        turned[...] = hidden[...].T
+
+    rows = out.shape[0]
+    out[...] = jnp.dot(turned[...], grads[...], preferred_element_type=jnp.float32)[:rows]
+
+    @pl.when(i == pl.num_programs(0) - 1)
+    def _():
+        for copy in copies:
+            copy.wait()
+
+
+def gathered(nodes, grad_out, gate_pre, up_pre, w_down):
+    tokens, hidden_units = gate_pre.shape
+    rows, width = grad_out.shape
+    levels = nodes // 2
+    block = hidden_units // nodes
+    padded = -(-block // LANES) * LANES
+    spread = max(k * block // LANES * LANES + padded + LANES for k in range(nodes))
+    everyone = nodes * 4 * rows
+    chunks = -(-hidden_units // STEP)
+    vmem, hbm = pl.BlockSpec(memory_space=pltpu.VMEM), pl.BlockSpec(memory_space=pl.ANY)
+    dma = pltpu.SemaphoreType.DMA
+    bf16 = jnp.bfloat16
+    all_grad, all_hidden, gg, gu = pl.pallas_call(
+        functools.partial(exchange, nodes),
+        out_shape=(
+            jax.ShapeDtypeStruct((everyone, width), bf16),
+            jax.ShapeDtypeStruct((nodes, tokens, padded), bf16),
+            jax.ShapeDtypeStruct(gate_pre.shape, bf16),
+            jax.ShapeDtypeStruct(gate_pre.shape, bf16),
+        ),
+        in_specs=[vmem, vmem, vmem, hbm],
+        out_specs=(hbm, hbm, vmem, vmem),
+        scratch_shapes=[
+            pltpu.VMEM(w_down.shape, bf16),
+            pltpu.VMEM((tokens, width), bf16),
+            pltpu.VMEM((tokens, spread), jnp.float32),
+            pltpu.VMEM((nodes, tokens, padded), bf16),
+        ] + [dma((levels,))] * 8 + [
+            dma((2, levels)), dma((levels,)),
+            dma((levels, 4)), dma((levels, 4)),
+            dma((nodes,)), dma((nodes,)),
+            dma((chunks,)), dma((3,)),
+        ],
+        compiler_params=pltpu.CompilerParams(
+            collective_id=0, has_side_effects=True, vmem_limit_bytes=56 * 1024 * 1024),
+        cost_estimate=pl.CostEstimate(
+            flops=2 * tokens * hidden_units * width, transcendentals=2 * tokens * hidden_units,
+            bytes_accessed=2 * w_down.size),
+        name="exchange",
+    )(grad_out, gate_pre, up_pre, w_down)
+
+    columns = 512
+    grad_weight, gg, gu = pl.pallas_call(
+        weight,
+        grid=(width // columns,),
+        out_shape=(
+            jax.ShapeDtypeStruct((block, width), jnp.float32),
+            jax.ShapeDtypeStruct(gate_pre.shape, bf16),
+            jax.ShapeDtypeStruct(gate_pre.shape, bf16),
+        ),
+        in_specs=[
+            pl.BlockSpec((everyone // 4 // rows * tokens, padded), lambda i: (0, 0)),
+            pl.BlockSpec((everyone, columns), lambda i: (0, i)),
+            hbm, hbm,
+        ],
+        out_specs=(pl.BlockSpec((block, columns), lambda i: (0, i)), hbm, hbm),
+        scratch_shapes=[pltpu.VMEM((padded, everyone), bf16), dma((2,))],
+        compiler_params=pltpu.CompilerParams(vmem_limit_bytes=48 * 1024 * 1024),
+        cost_estimate=pl.CostEstimate(
+            flops=2 * everyone * padded * width, transcendentals=0,
+            bytes_accessed=2 * everyone * width + 4 * block * width),
+        name="weight",
+    )(all_hidden.reshape(nodes * tokens, padded), all_grad, gg, gu)
+    return gg, gu, grad_weight
+
+
 def solution(mesh):
+    nodes, local = mesh.shape["node"], mesh.shape["local"]
+    devices = nodes * local
+
+    def on_device(grad_out, gate_pre, up_pre, w_down):
+        gather_bytes = devices * grad_out.size * 2
+        sum_bytes = w_down.size * 4
+        fits = local == 4 and nodes % 2 == 0 and grad_out.shape[0] % 16 == 0
+        if fits and gather_bytes < sum_bytes and w_down.size <= 2 ** 24:
+            return gathered(nodes, grad_out, gate_pre, up_pre, w_down)
+        return summed(grad_out, gate_pre, up_pre, w_down)
+
     return jax.shard_map(
         on_device,
         mesh=mesh,

time: 622 us -> 58.1 us (0.09)
  waiting for transfers between devices: 555 us -> 0 us
  Pallas kernels: 0 us -> 51.8 us
  matrix products: 40.1 us -> 0 us
  between operations: 14 us -> 0.65 us
  blocking collectives: 11.8 us -> 0 us
    unnamed x2 -> x0, waiting for transfers between devices: 555 us -> none
    pallas_call x0 -> x2, Pallas kernels: none -> 51.8 us  [the longest x1 45.5 us: gathered(): pl.pallas_call(functools.partial(exchange, nodes), out_shape=(jax.ShapeDt...]
    dot_general x2 -> x0, matrix products: 40.1 us -> none  [the longest x1 24.1 us: on_device(): jnp.einsum('tf,td->fd', hidden, node_grad, preferred_element_type=jnp.flo...]
    all_gather x1 -> x0, blocking collectives: 11.8 us -> none  [on_device(): node_grad = lax.all_gather(grad_out, 'local', axis=0, tiled=True)]
  transfers between devices with their start and end apart: 1 -> 0, of which waited for: 1 -> 0; matrix products, arithmetic and copies ran while one was open for 3% -> 0% of each run, Pallas kernels for 0% -> 0%
where the time goes in v2:
time: 58.1 us; the launch traced here: 57.7 us
  Pallas kernels  51.8 us (89%)
  local copies, waits for them, and re-layouts  5.27 us (9%)
  between operations  0.65 us (1%)
    pallas_call x1, Pallas kernels, gathered(): pl.pallas_call(functools.partial(exchange, nodes), out_shape=(jax.ShapeDt...  45.5 us
    pallas_call x1, Pallas kernels, gathered(): pl.pallas_call(weight, grid=(width // columns,), out_shape=(jax.ShapeDtyp...  6.34 us
    unnamed x8, local copies, waits for them, and re-layouts  5.27 us

profile of v2, /device:TPU:0, one launch (start us, length us, event | category | flops | bytes accessed | tf_op | source)
XLA Modules:
  0.0 57.7 jit_solution(3778888133965792456)
XLA Ops:
  0.6 45.5 %exchange.1 = (bf16[512,4096]{1,0:T(8,128)(2,1)}, bf16[8,64,512]{2,1,0:T(8,128)(2,1)}, bf16[64,3648]{1,0:T(8,128)(2,1)}, bf16[64,3648]{1,0:T(8,128)(2,1)}) custom-call(bf16[16,4096]{1,0:T(8,128)(2,1)} %go.1, bf16[64,3648]{1,0:T(8,128)(2,1)} %gate.1, bf16[64,3648]{1,0:T(8,128)(2,1)} %up.1, bf16[3648,4096]{1,0:T(8,128)(2,1)} %w.1), custom_call_target="tpu_custom_call" | custom-call | flops 1912602624 | bytes 29884416 | tf_op jit(solution)/shard_map/exchange/pallas_call | solution.py:268
  46.1 0.0 copy-start
  46.1 2.2 %copy-done = bf16[512,4096]{1,0:T(8,128)(2,1)S(1)} copy-done((bf16[512,4096]{1,0:T(8,128)(2,1)S(1)}, bf16[512,4096]{1,0:T(8,128)(2,1)}, u32[]{:S(2)}) %copy-start) | copy-done | bytes 4194328
  48.3 0.0 copy-start.1
  48.3 1.0 %copy-done.1 = bf16[8,64,512]{2,1,0:T(8,128)(2,1)S(1)} copy-done((bf16[8,64,512]{2,1,0:T(8,128)(2,1)S(1)}, bf16[8,64,512]{2,1,0:T(8,128)(2,1)}, u32[]{:S(2)}) %copy-start.1) | copy-done | bytes 524312
  49.3 0.0 copy-start.2
  49.3 1.0 %copy-done.2 = bf16[64,3648]{1,0:T(8,128)(2,1)S(1)} copy-done((bf16[64,3648]{1,0:T(8,128)(2,1)S(1)}, bf16[64,3648]{1,0:T(8,128)(2,1)}, u32[]{:S(2)}) %copy-start.2) | copy-done | bytes 466968
  50.3 0.0 copy-start.3
  50.4 1.0 %copy-done.3 = bf16[64,3648]{1,0:T(8,128)(2,1)S(1)} copy-done((bf16[64,3648]{1,0:T(8,128)(2,1)S(1)}, bf16[64,3648]{1,0:T(8,128)(2,1)}, u32[]{:S(2)}) %copy-start.3) | copy-done | bytes 466968
  51.4 6.3 %weight.1 = (f32[456,4096]{1,0:T(8,128)}, bf16[64,3648]{1,0:T(8,128)(2,1)}, bf16[64,3648]{1,0:T(8,128)(2,1)}) custom-call(bf16[512,512]{1,0:T(8,128)(2,1)S(1)} %bitcast.1, bf16[512,4096]{1,0:T(8,128)(2,1)S(1)} %copy-done, bf16[64,3648]{1,0:T(8,128)(2,1)S(1)} %copy-done.2, bf16[64,3648]{1,0:T(8,128)(2,1)S(1)} %copy-done.3), custom_call_target="tpu_custom_call" | custom-call | flops 2147483648 | bytes 11665408 | tf_op jit(solution)/shard_map/weight/pallas_call | solution.py:298
Async XLA Ops:
  46.1 2.2 %copy-start = (bf16[512,4096]{1,0:T(8,128)(2,1)S(1)}, bf16[512,4096]{1,0:T(8,128)(2,1)}, u32[]{:S(2)}) copy-start(bf16[512,4096]{1,0:T(8,128)(2,1)} %get-tuple-element.11.grads) | copy-start | bytes 12582916
  48.3 1.0 %copy-start.1 = (bf16[8,64,512]{2,1,0:T(8,128)(2,1)S(1)}, bf16[8,64,512]{2,1,0:T(8,128)(2,1)}, u32[]{:S(2)}) copy-start(bf16[8,64,512]{2,1,0:T(8,128)(2,1)} %get-tuple-element.10) | copy-start | bytes 1572868
  49.3 1.0 %copy-start.2 = (bf16[64,3648]{1,0:T(8,128)(2,1)S(1)}, bf16[64,3648]{1,0:T(8,128)(2,1)}, u32[]{:S(2)}) copy-start(bf16[64,3648]{1,0:T(8,128)(2,1)} %get-tuple-element.12.gg) | copy-start | bytes 1400836
  50.3 1.0 %copy-start.3 = (bf16[64,3648]{1,0:T(8,128)(2,1)S(1)}, bf16[64,3648]{1,0:T(8,128)(2,1)}, u32[]{:S(2)}) copy-start(bf16[64,3648]{1,0:T(8,128)(2,1)} %get-tuple-element.13.gu) | copy-start | bytes 1400836

commit v3 on v2

--- a/solution.py
+++ b/solution.py
@@ -31,8 +31,8 @@
     return (grad_gate, grad_up, grad_weight)
 
 
-def exchange(nodes, go, gate, up, w, all_grad, all_hidden, gg, gu,
-             wv, ng, hf, hs, xs, xr, ys, yr, xhs, xhr, yhs, yhr, zs, zr, ss, sr, hss, hsr, ws, ls):
+def exchange(nodes, go_in, gate_in, up_in, w, all_grad, all_hidden, gg_out, gu_out,
+             go, gate, up, gg, gu, wv, ng, hf, hs, xs, xr, ys, yr, xhs, xhr, yhs, yhr, zs, zr, ss, sr, hss, hsr, ws, ls):
     n, l = lax.axis_index("node"), lax.axis_index("local")
     levels = nodes // 2
     z, c = lax.div(n, 2), lax.rem(n, 2)
@@ -45,6 +45,12 @@
     block = hidden_units // nodes
     padded = hs.shape[2]
 
+    first = pltpu.make_async_copy(go_in, go, ls.at[7])
+    first.start()
+    loads = [pltpu.make_async_copy(gate_in, gate, ls.at[3]), pltpu.make_async_copy(up_in, up, ls.at[4])]
+    for copy in loads:
+        copy.start()
+
     starts = list(range(0, hidden_units, STEP))
     full = hidden_units // STEP
 
@@ -129,11 +135,15 @@
         arrived(slot(level, c, ld, 1), xhr.at[level])
         from_d(level, start)
 
+    first.wait()
     for side in (-1, 1):
         along(z, go, side, start)
     across(z, go, start)
     own = pltpu.make_async_copy(go, slot(z, c, l), ls.at[0])
     own.start()
+
+    for copy in loads:
+        copy.wait()
 
     spread = hf.shape[1]
     last = hidden_units // LANES * LANES
@@ -164,8 +174,6 @@
         to = lax.rem(n + k, nodes)
         return remote(hs.at[to], all_hidden.at[n], hss.at[k], hsr.at[n], (to, l))
 
-    for k in range(1, nodes):
-        hidden_copy(k).start()
     own_hidden = pltpu.make_async_copy(hs.at[n], all_hidden.at[n], ls.at[1])
     own_hidden.start()
 
@@ -186,9 +194,9 @@
         def _(i):
             multiply(i)
 
-    xy_event(z)
     if levels > 1:
         each(1, z_event)
+    xy_event(z)
     d_event(z)
     own.wait()
     node_rows = pl.ds(pl.multiple_of(n * tokens, tokens), tokens)
@@ -200,12 +208,20 @@
         multiply_some(2 * distance - 2, parts)
         if distance + 1 < levels:
             each(distance + 1, z_event)
+        for k in range(1 + (distance - 1) * nodes // levels, 1 + distance * nodes // levels):
+            hidden_copy(k).start()
         each(distance, xy_event)
         multiply_some(2 * distance - 1, parts)
         each(distance, d_event)
+    for k in range(1 + (levels - 1) * nodes // levels, nodes):
+        hidden_copy(k).start()
     multiply_some(parts - 1, parts)
     if hidden_units % STEP:
         multiply(full, hidden_units % STEP)
+
+    stores = [pltpu.make_async_copy(gg, gg_out, ls.at[5]), pltpu.make_async_copy(gu, gu_out, ls.at[6])]
+    for copy in stores:
+        copy.start()
 
     @pl.loop(0, levels)
     def _(level):
@@ -217,6 +233,8 @@
         arrived(all_hidden.at[other], hsr.at[other])
         hidden_copy(k).wait_send()
     own_hidden.wait()
+    for copy in stores:
+        copy.wait()
 
     def z_sent(level, side):
         along(level, slot(level, c, l), -side, sent)
@@ -262,7 +280,7 @@
     spread = max(k * block // LANES * LANES + padded + LANES for k in range(nodes))
     everyone = nodes * 4 * rows
     chunks = -(-hidden_units // STEP)
-    vmem, hbm = pl.BlockSpec(memory_space=pltpu.VMEM), pl.BlockSpec(memory_space=pl.ANY)
+    hbm = pl.BlockSpec(memory_space=pl.ANY)
     dma = pltpu.SemaphoreType.DMA
     bf16 = jnp.bfloat16
     all_grad, all_hidden, gg, gu = pl.pallas_call(
@@ -273,9 +291,9 @@
             jax.ShapeDtypeStruct(gate_pre.shape, bf16),
             jax.ShapeDtypeStruct(gate_pre.shape, bf16),
         ),
-        in_specs=[vmem, vmem, vmem, hbm],
-        out_specs=(hbm, hbm, vmem, vmem),
-        scratch_shapes=[
+        in_specs=[hbm] * 4,
+        out_specs=(hbm,) * 4,
+        scratch_shapes=[pltpu.VMEM(grad_out.shape, bf16)] + [pltpu.VMEM(gate_pre.shape, bf16)] * 4 + [
             pltpu.VMEM(w_down.shape, bf16),
             pltpu.VMEM((tokens, width), bf16),
             pltpu.VMEM((tokens, spread), jnp.float32),
@@ -284,7 +302,7 @@
             dma((2, levels)), dma((levels,)),
             dma((levels, 4)), dma((levels, 4)),
             dma((nodes,)), dma((nodes,)),
-            dma((chunks,)), dma((3,)),
+            dma((chunks,)), dma((8,)),
         ],
         compiler_params=pltpu.CompilerParams(
             collective_id=0, has_side_effects=True, vmem_limit_bytes=56 * 1024 * 1024),
@@ -294,7 +312,7 @@
         name="exchange",
     )(grad_out, gate_pre, up_pre, w_down)
 
-    columns = 512
+    columns = 2048
     grad_weight, gg, gu = pl.pallas_call(
         weight,
         grid=(width // columns,),
@@ -306,11 +324,12 @@
         in_specs=[
             pl.BlockSpec((everyone // 4 // rows * tokens, padded), lambda i: (0, 0)),
             pl.BlockSpec((everyone, columns), lambda i: (0, i)),
-            hbm, hbm,
+            pl.BlockSpec(gate_pre.shape, lambda i: (0, 0)),
+            pl.BlockSpec(gate_pre.shape, lambda i: (0, 0)),
         ],
         out_specs=(pl.BlockSpec((block, columns), lambda i: (0, i)), hbm, hbm),
         scratch_shapes=[pltpu.VMEM((padded, everyone), bf16), dma((2,))],
-        compiler_params=pltpu.CompilerParams(vmem_limit_bytes=48 * 1024 * 1024),
+        compiler_params=pltpu.CompilerParams(vmem_limit_bytes=60 * 1024 * 1024),
         cost_estimate=pl.CostEstimate(
             flops=2 * everyone * padded * width, transcendentals=0,
             bytes_accessed=2 * everyone * width + 4 * block * width),

time: 58.1 us -> 52.1 us (0.90)
  local copies, waits for them, and re-layouts: 5.27 us -> 0 us
    unnamed x8 -> x0, local copies, waits for them, and re-layouts: 5.27 us -> none
    pallas_call x1, Pallas kernels: 45.5 us -> 44.7 us  [gathered(): pl.pallas_call(functools.partial(exchange, nodes), out_shape=(jax.ShapeDt...]
where the time goes in v3:
time: 52.1 us; the launch traced here: 51.9 us
  Pallas kernels  51.3 us (98%)
  between operations  0.64 us (1%)
    pallas_call x1, Pallas kernels, gathered(): pl.pallas_call(functools.partial(exchange, nodes), out_shape=(jax.ShapeDt...  44.7 us
    pallas_call x1, Pallas kernels, gathered(): pl.pallas_call(weight, grid=(width // columns,), out_shape=(jax.ShapeDtyp...  6.6 us

profile of v3, /device:TPU:0, one launch (start us, length us, event | category | flops | bytes accessed | tf_op | source)
XLA Modules:
  0.0 51.9 jit_solution(2527236466028497038)
XLA Ops:
  0.6 44.7 %exchange.1 = (bf16[512,4096]{1,0:T(8,128)(2,1)}, bf16[8,64,512]{2,1,0:T(8,128)(2,1)}, bf16[64,3648]{1,0:T(8,128)(2,1)}, bf16[64,3648]{1,0:T(8,128)(2,1)}) custom-call(bf16[16,4096]{1,0:T(8,128)(2,1)} %go_in.1, bf16[64,3648]{1,0:T(8,128)(2,1)} %gate_in.1, bf16[64,3648]{1,0:T(8,128)(2,1)} %up_in.1, bf16[3648,4096]{1,0:T(8,128)(2,1)} %w.1), custom_call_target="tpu_custom_call" | custom-call | flops 1912602624 | bytes 29884416 | tf_op jit(solution)/shard_map/exchange/pallas_call | solution.py:286
  45.3 6.6 %weight.1 = (f32[456,4096]{1,0:T(8,128)}, bf16[64,3648]{1,0:T(8,128)(2,1)}, bf16[64,3648]{1,0:T(8,128)(2,1)}) custom-call(bf16[512,512]{1,0:T(8,128)(2,1)} %bitcast.1, bf16[512,4096]{1,0:T(8,128)(2,1)} %get-tuple-element.11.grads, bf16[64,3648]{1,0:T(8,128)(2,1)} %get-tuple-element.12.gg, bf16[64,3648]{1,0:T(8,128)(2,1)} %get-tuple-element.13.gu), custom_call_target="tpu_custom_call" | custom-call | flops 2147483648 | bytes 11665408 | tf_op jit(solution)/shard_map/weight/pallas_call | solution.py:316

commit v4 on v3

--- a/solution.py
+++ b/solution.py
@@ -208,17 +208,19 @@
         multiply_some(2 * distance - 2, parts)
         if distance + 1 < levels:
             each(distance + 1, z_event)
-        for k in range(1 + (distance - 1) * nodes // levels, 1 + distance * nodes // levels):
+        final = distance + 1 == levels
+        for k in range(1 + (distance - 1) * nodes // levels, nodes if final else 1 + distance * nodes // levels):
             hidden_copy(k).start()
+        if final:
+            multiply_some(2 * distance - 1, parts)
         each(distance, xy_event)
-        multiply_some(2 * distance - 1, parts)
+        if final:
+            multiply_some(parts - 1, parts)
+            if hidden_units % STEP:
+                multiply(full, hidden_units % STEP)
+        else:
+            multiply_some(2 * distance - 1, parts)
         each(distance, d_event)
-    for k in range(1 + (levels - 1) * nodes // levels, nodes):
-        hidden_copy(k).start()
-    multiply_some(parts - 1, parts)
-    if hidden_units % STEP:
-        multiply(full, hidden_units % STEP)
-
     stores = [pltpu.make_async_copy(gg, gg_out, ls.at[5]), pltpu.make_async_copy(gu, gu_out, ls.at[6])]
     for copy in stores:
         copy.start()
@@ -345,7 +347,7 @@
     def on_device(grad_out, gate_pre, up_pre, w_down):
         gather_bytes = devices * grad_out.size * 2
         sum_bytes = w_down.size * 4
-        fits = local == 4 and nodes % 2 == 0 and grad_out.shape[0] % 16 == 0
+        fits = local == 4 and nodes % 2 == 0 and nodes > 2 and grad_out.shape[0] % 16 == 0
         if fits and gather_bytes < sum_bytes and w_down.size <= 2 ** 24:
             return gathered(nodes, grad_out, gate_pre, up_pre, w_down)
         return summed(grad_out, gate_pre, up_pre, w_down)

time: 52.1 us -> 50.9 us (0.977)
  Pallas kernels: 51.3 us -> 50.1 us
    pallas_call x1, Pallas kernels: 44.7 us -> 43.5 us  [gathered(): pl.pallas_call(functools.partial(exchange, nodes), out_shape=(jax.ShapeDt...]
where the time goes in v4:
time: 50.9 us; the launch traced here: 50.7 us
  Pallas kernels  50.1 us (98%)
  between operations  0.64 us (1%)
    pallas_call x1, Pallas kernels, gathered(): pl.pallas_call(functools.partial(exchange, nodes), out_shape=(jax.ShapeDt...  43.5 us
    pallas_call x1, Pallas kernels, gathered(): pl.pallas_call(weight, grid=(width // columns,), out_shape=(jax.ShapeDtyp...  6.6 us

profile of v4, /device:TPU:0, one launch (start us, length us, event | category | flops | bytes accessed | tf_op | source)
XLA Modules:
  0.0 50.7 jit_solution(16333861374872396076)
XLA Ops:
  0.6 43.5 %exchange.1 = (bf16[512,4096]{1,0:T(8,128)(2,1)}, bf16[8,64,512]{2,1,0:T(8,128)(2,1)}, bf16[64,3648]{1,0:T(8,128)(2,1)}, bf16[64,3648]{1,0:T(8,128)(2,1)}) custom-call(bf16[16,4096]{1,0:T(8,128)(2,1)} %go_in.1, bf16[64,3648]{1,0:T(8,128)(2,1)} %gate_in.1, bf16[64,3648]{1,0:T(8,128)(2,1)} %up_in.1, bf16[3648,4096]{1,0:T(8,128)(2,1)} %w.1), custom_call_target="tpu_custom_call" | custom-call | flops 1912602624 | bytes 29884416 | tf_op jit(solution)/shard_map/exchange/pallas_call | solution.py:288
  44.1 6.6 %weight.1 = (f32[456,4096]{1,0:T(8,128)}, bf16[64,3648]{1,0:T(8,128)(2,1)}, bf16[64,3648]{1,0:T(8,128)(2,1)}) custom-call(bf16[512,512]{1,0:T(8,128)(2,1)} %bitcast.1, bf16[512,4096]{1,0:T(8,128)(2,1)} %get-tuple-element.11.grads, bf16[64,3648]{1,0:T(8,128)(2,1)} %get-tuple-element.12.gg, bf16[64,3648]{1,0:T(8,128)(2,1)} %get-tuple-element.13.gu), custom_call_target="tpu_custom_call" | custom-call | flops 2147483648 | bytes 11665408 | tf_op jit(solution)/shard_map/weight/pallas_call | solution.py:318
